TPU v7x, 128 devices: a whole 4x4x4 slice. The times are simulated.
128 devices in a mesh: db: 4 (over z), seq: 32 (over x, y, core).
Axes of the slice: x: 4, y: 4, z: 4, core: 2. Of those that a mesh axis runs over, the one named last changes fastest.
Arguments:
- queries: bfloat16 [16384, 4096], P(('db', 'seq')), may hold values from -250 to 250
- encoded: bfloat16 [64, 128, 1024], P('db'), may hold values from -6 to 6
- key_weight: bfloat16 [1024, 4096], replicated, may hold values from -0.1875 to 0.1875
- value_weight: bfloat16 [1024, 4096], replicated, may hold values from -0.1875 to 0.1875
- nbr_shard: int32 [256, 2], P(('db', 'seq')), may hold values from 0 to 3, all different within a row; in each aligned block of 2 rows (0 to 1, 2 to 3, ...) at most 2 rows name the same one
- nbr_slot: int32 [256, 2], P(('db', 'seq')), may hold values from 0 to 15
Outputs:
- attended: bfloat16 [16384, 4096], P(('db', 'seq'))
Inputs may be any that keep to these rules, and one draw needn't show every extreme that they name: `nbr_shard`: the 2 neighbours of one group lie in different shards; the neighbours of the groups of one device lie at most 2 in one shard, and exactly 2 in one shard for some device.
All inputs are finite; a program needn't handle non-finite values.
Results may differ from a plain program's by a relative error of at most 0.012.
The roundings to bfloat16 on the way count: a program that leaves them out, or rounds other values in their place, can miss the bound.
Values may be sent and summed in bfloat16 or wider, within the bound.
A program may use at most 128 MiB of HBM per device.

v0:
```python
import math

import jax
import jax.numpy as jnp
from jax import lax
from jax.sharding import PartitionSpec as P

H = 32
HD = 128
DE = 1024
CL = 64
NB = 2
NT = 128
LENGTH = 2048


def from_behind(value, axis, steps):
    count = lax.axis_size(axis)
    leading, last = (max(0, -steps), min(count, count - steps))
    return lax.ppermute(value, axis, [(source, source + steps) for source in range(leading, last)])


def project(rows, key_weight, value_weight):
    count = rows.shape[0]
    flat = rows.reshape(count * NB * NT, DE)
    keys = jnp.dot(flat, key_weight, preferred_element_type=jnp.float32).astype(jnp.bfloat16)
    values = jnp.dot(flat, value_weight, preferred_element_type=jnp.float32).astype(jnp.bfloat16)
    width = key_weight.shape[1]
    return (keys.reshape(count, NB * NT, width), values.reshape(count, NB * NT, width))


def body(queries, encoded, key_weight, value_weight, nbr_shard, nbr_slot):
    tok_rows, width = queries.shape
    per_dev = nbr_shard.shape[0]
    shards = lax.axis_size("db")
    capacity = max(2, (per_dev * NB + shards - 1) // shards)
    owner = nbr_shard.reshape(-1)
    places = nbr_slot.reshape(-1)
    count = owner.shape[0]
    order = jnp.arange(count, dtype=jnp.int32)
    earlier = order[None, :] < order[:, None]
    same = owner[None, :] == owner[:, None]
    rank = jnp.sum(jnp.where(same & earlier, 1, 0), axis=1).astype(jnp.int32)
    target = owner * capacity + rank
    buffer_slots = jnp.arange(shards * capacity, dtype=jnp.int32)
    hits = target[None, :] == buffer_slots[:, None]
    requests = jnp.sum(jnp.where(hits, places[None, :], 0), axis=1)
    requests = requests.reshape(shards, capacity)
    found = jnp.take(
        encoded, lax.all_to_all(requests, "db", split_axis=0, concat_axis=0, tiled=True), axis=0
    )
    returned = lax.all_to_all(found, "db", split_axis=0, concat_axis=0, tiled=True)
    picked = jnp.take(returned.reshape(shards * capacity, NT, DE), target, axis=0)
    picked = picked.reshape(per_dev, NB * NT, DE)
    keys, values = project(picked, key_weight, value_weight)
    stacked = jnp.stack([keys[-1], values[-1]])
    arrived = from_behind(stacked, ("db", "seq"), 1)
    prev_keys = arrived[0][None]
    prev_values = arrived[1][None]
    all_keys = jnp.concatenate([prev_keys, keys], axis=0).reshape(per_dev + 1, NB * NT, H, HD)
    all_values = jnp.concatenate([prev_values, values], axis=0).reshape(per_dev + 1, NB * NT, H, HD)
    front = jnp.zeros((1, width), queries.dtype)
    back = jnp.zeros((CL - 1, width), queries.dtype)
    padded_q = jnp.concatenate([front, queries, back], axis=0).reshape(per_dev + 1, CL, H, HD)
    scores = jnp.einsum(
        "bqhd,bkhd->bhqk", padded_q, all_keys, preferred_element_type=jnp.float32
    ) / math.sqrt(HD)
    weights = jax.nn.softmax(scores, axis=-1).astype(jnp.bfloat16)
    mixed = jnp.einsum("bhqk,bkhd->bqhd", weights, all_values, preferred_element_type=jnp.float32)
    mixed = mixed.astype(jnp.bfloat16).reshape((per_dev + 1) * CL, width)
    result = mixed[1 : tok_rows + 1]
    start = lax.axis_index(("db", "seq")) * tok_rows
    position = (start + jnp.arange(tok_rows, dtype=jnp.int32)) % LENGTH
    blank = jnp.zeros_like(result)
    return jnp.where((position < CL - 1)[:, None], blank, result)


def solution(mesh):
    placed = (
        P(("db", "seq"), None),
        P("db", None, None),
        P(),
        P(),
        P(("db", "seq"), None),
        P(("db", "seq"), None),
    )
    return jax.shard_map(
        body, mesh=mesh, in_specs=placed, out_specs=P(("db", "seq"), None), check_vma=False
    )
```

profile of v0, /device:TPU:32, one launch (start us, length us, event | category | flops | bytes accessed | tf_op | source)
XLA Modules:
  0.0 149.7 jit_solution(9292773036668922538)
XLA Ops:
  0.0 0.8 broadcast_in_dim.77
  0.8 0.8 reshape.128
  1.9 9.0 %all_to_all.20 = s32[4,1,2]{2,1,0:T(1,128)S(1)} all-to-all(s32[4,1,2]{2,1,0:T(1,128)S(1)} %bitcast.66), channel_id=1, replica_groups=mesh['db'=4,'seq'=32] {'db'}, dimensions={0} | all-to-all | bytes 64 | tf_op jit(solution)/shard_map/all_to_all | solution.py:50
  11.3 2.9 %gather_fusion = bf16[8,128,1024]{2,1,0:T(8,128)(2,1)S(1)} fusion(bf16[16,128,1024]{2,1,0:T(8,128)(2,1)} %param.7, s32[1024]{0:T(1024)S(1)} %pad_clamp_fusion.1), kind=kCustom, calls=%fused_computation | custom fusion | bytes 4194336 | tf_op jit(solution)/shard_map/jit(_take)/gather | solution.py:49
  14.2 1.6 %broadcast_select_fusion = bf16[4,2,128,1024]{3,2,1,0:T(8,128)(2,1)} fusion(bf16[4,2,128,1024]{3,2,1,0:T(8,128)(2,1)S(1)} %bitcast.60, pred[4,2]{1,0:T(4,128)(4,1)S(1)} %copy.38), kind=kLoop, calls=%fused_computation.26 | loop fusion | flops 1048576 | bytes 4194312 | tf_op jit(solution)/shard_map/jit(_take)/select_n | solution.py:49
  15.8 5.0 %all-to-all-start.1 = ((bf16[4,2,128,1024]{3,2,1,0:T(8,128)(2,1)}), bf16[4,2,128,1024]{3,2,1,0:T(8,128)(2,1)S(1)}, u32[]{:S(2)}, u32[]{:S(2)}) async-start(bf16[4,2,128,1024]{3,2,1,0:T(8,128)(2,1)} %broadcast_select_fusion), calls=%async_computation.1 | async-start | bytes 4194304 | tf_op jit(solution)/shard_map/all_to_all | solution.py:52
  21.0 23.5 %all-to-all-done.1 = bf16[4,2,128,1024]{3,2,1,0:T(8,128)(2,1)S(1)} async-done(((bf16[4,2,128,1024]{3,2,1,0:T(8,128)(2,1)}), bf16[4,2,128,1024]{3,2,1,0:T(8,128)(2,1)S(1)}, u32[]{:S(2)}, u32[]{:S(2)}) %all-to-all-start.1) | async-done | bytes 2097184 | tf_op jit(solution)/shard_map/all_to_all | solution.py:52
  44.5 0.6 gather_fusion.1
  45.2 0.2 bitcast_select_fusion
  45.4 8.3 %convolution_convert_fusion = bf16[512,4096]{1,0:T(8,128)(2,1)S(1)} fusion(bf16[512,1024]{1,0:T(8,128)(2,1)S(1)} %bitcast_select_fusion, bf16[1024,4096]{1,0:T(8,128)(2,1)} %param.9), kind=kOutput, calls=%fused_computation.13 | convolution fusion | flops 4297064448 | bytes 13631488 | tf_op jit(solution)/shard_map/dot_general | solution.py:27
  53.7 4.8 %convolution_convert_fusion.1 = bf16[512,4096]{1,0:T(8,128)(2,1)S(1)} fusion(bf16[512,1024]{1,0:T(8,128)(2,1)S(1)} %bitcast_select_fusion, bf16[1024,4096]{1,0:T(8,128)(2,1)S(1)} %bitcast.68), kind=kOutput, calls=%fused_computation.14 | convolution fusion | flops 4297064448 | bytes 13631488 | tf_op jit(solution)/shard_map/dot_general | solution.py:26
  58.5 0.5 slice_bitcast_fusion.2
  59.0 1.4 copy-done
  60.5 2.3 %pad_maximum_fusion = bf16[2,256,4096]{2,1,0:T(8,128)(2,1)} fusion(bf16[1,256,4096]{2,1,0:T(8,128)(2,1)S(1)} %get-tuple-element.9, bf16[1,256,4096]{2,1,0:T(8,128)(2,1)S(1)} %get-tuple-element.10), kind=kLoop, calls=%fused_computation.17 | loop fusion | flops 2097152 | bytes 8388608 | tf_op jit(solution)/shard_map/stack | solution.py:56
  62.8 2.1 %collective-permute-start = (bf16[2,256,4096]{2,1,0:T(8,128)(2,1)}, bf16[2,256,4096]{2,1,0:T(8,128)(2,1)}, u32[]{:S(2)}, u32[]{:S(2)}) collective-permute-start(bf16[2,256,4096]{2,1,0:T(8,128)(2,1)} %pad_maximum_fusion), channel_id=1, source_target_pairs={{0,1},{1,2},{2,3},{3,4},{4,5},{5,6},{6,7},{7,8},{8,9},{9,10},{10,1... | collective-permute-start | bytes 12582920 | tf_op jit(solution)/shard_map/ppermute | solution.py:20
  65.0 0.5 maximum_bitcast_fusion
  65.5 0.3 copy.49
  65.9 3.4 %copy.51 = bf16[64,8,32,128]{3,2,1,0:T(8,128)(2,1)S(1)} copy(bf16[64,8,32,128]{3,1,2,0:T(8,128)(2,1)} %bitcast.58) | data formatting | bytes 8388608
  69.3 3.6 %copy.42 = bf16[2,256,32,128]{3,1,2,0:T(8,128)(2,1)} copy(bf16[2,256,32,128]{3,2,1,0:T(8,128)(2,1)S(1)} %bitcast.55) | data formatting | bytes 8388608 | tf_op jit(solution)/shard_map/concatenate | solution.py:61
  72.9 1.3 copy.50
  74.2 1.6 %copy.44 = bf16[2,256,32,128]{3,1,2,0:T(8,128)(2,1)S(1)} copy(bf16[2,256,32,128]{3,2,1,0:T(8,128)(2,1)S(1)} %bitcast.56) | data formatting | bytes 8388608 | tf_op jit(solution)/shard_map/concatenate | solution.py:60
  75.8 41.4 %collective-permute-done = bf16[2,256,4096]{2,1,0:T(8,128)(2,1)} collective-permute-done((bf16[2,256,4096]{2,1,0:T(8,128)(2,1)}, bf16[2,256,4096]{2,1,0:T(8,128)(2,1)}, u32[]{:S(2)}, u32[]{:S(2)}) %collective-permute-start) | collective-permute-done | bytes 4194336 | tf_op jit(solution)/shard_map/ppermute | solution.py:20
  117.1 2.7 %slice_bitcast_fusion.1 = (bf16[1,32,32,8,128]{4,3,2,1,0:T(8,128)(2,1)S(1)}, bf16[1,32,32,8,128]{4,3,2,1,0:T(8,128)(2,1)S(1)}) fusion(bf16[2,256,4096]{2,1,0:T(8,128)(2,1)} %collective-permute-done), kind=kLoop, calls=%fused_computation.23 | loop fusion | bytes 8388608
  119.8 1.9 %copy.58 = bf16[1,32,32,8,128]{4,3,1,2,0:T(8,128)(2,1)} copy(bf16[1,32,32,8,128]{4,3,2,1,0:T(8,128)(2,1)S(1)} %get-tuple-element.8) | data formatting | bytes 4194304 | tf_op jit(solution)/shard_map/concatenate | solution.py:61
  121.7 0.6 copy.59
  122.3 2.6 %fusion.1 = f32[3,32,64,256]{3,2,1,0:T(8,128)S(1)} fusion(bf16[2,256,32,128]{3,1,2,0:T(8,128)(2,1)S(1)} %copy.44, bf16[1,256,32,128]{3,1,2,0:T(8,128)(2,1)S(1)} %bitcast.59, bf16[3,64,32,128]{3,2,1,0:T(8,128)(2,1)S(1)} %bitcast.61), kind=kOutput, calls=%fused_computation.3 | convolution fusion | flops 405798912 | bytes 14155776 | tf_op jit(solution)/shard_map/bqhd,bkhd->bhqk/dot_general | solution.py:65
  124.9 2.6 %copy-done.3 = f32[3,32,64,256]{3,2,1,0:T(8,128)} copy-done((f32[3,32,64,256]{3,2,1,0:T(8,128)}, f32[3,32,64,256]{3,2,1,0:T(8,128)S(1)}, u32[]{:S(2)}) %copy-start.3) | copy-done | bytes 6291480
  127.6 2.4 %fusion.35 = f32[3,32,64]{2,1,0:T(8,128)S(1)} fusion(f32[3,32,64,256]{3,2,1,0:T(8,128)S(1)} %fusion.1), kind=kOutput, calls=%fused_computation.62 | output fusion | flops 6291711 | bytes 6316032 | tf_op jit(solution)/shard_map/sub | solution.py:68
  130.0 15.3 %fusion.18 = bf16[3,64,32,128]{3,1,2,0:T(8,128)(2,1)} fusion(bf16[2,256,32,128]{3,1,2,0:T(8,128)(2,1)} %copy.42, bf16[1,256,32,128]{3,1,2,0:T(8,128)(2,1)S(1)} %bitcast.65, f32[3,32,64]{2,1,0:T(8,128)S(1)} %fusion.35, f32[3,32,64,256]{3,2,1,0:T(8,128)} %copy-done.3), kind=kOutput, calls=%fused_computation.31 | convolution fusion | flops 423893248 | bytes 14180352 | tf_op jit(solution)/shard_map/bhqk,bkhd->bqhd/dot_general | solution.py:69
  145.3 2.4 %copy.46 = bf16[3,64,32,128]{3,2,1,0:T(8,128)(2,1)S(1)} copy(bf16[3,64,32,128]{3,1,2,0:T(8,128)(2,1)} %fusion.18) | data formatting | bytes 3145728 | tf_op jit(solution)/shard_map/convert_element_type | solution.py:70
  147.7 0.7 copy.60
  148.4 1.3 slice_select_fusion
  (37 shorter events, 1.1 us)
Async XLA Ops:
  14.2 6.7 %copy-start.6 = (s32[2,2]{1,0:T(2,128)S(1)}, s32[2,2]{1,0:T(2,128)}, u32[]{:S(2)}) copy-start(s32[2,2]{1,0:T(2,128)} %param.10) | copy-start | bytes 52
  15.8 28.8 %all-to-all-start.1 = ((bf16[4,2,128,1024]{3,2,1,0:T(8,128)(2,1)}), bf16[4,2,128,1024]{3,2,1,0:T(8,128)(2,1)S(1)}, u32[]{:S(2)}, u32[]{:S(2)}) async-start(bf16[4,2,128,1024]{3,2,1,0:T(8,128)(2,1)} %broadcast_select_fusion), calls=%async_computation.1 | async-start | bytes 4194304 | tf_op jit(solution)/shard_map/all_to_all | solution.py:52
  45.2 8.5 %slice-start = ((s8[8388608]{0:T(1024)(128)(4,1)}), s8[4194304]{0:T(1024)(128)(4,1)S(1)}, s32[]{:S(2)}) async-start(s8[8388608]{0:T(1024)(128)(4,1)} %bitcast.67), calls=%async_computation.2 | async-start | bytes 8388608
  45.4 8.3 %slice-start.1 = ((s8[8388608]{0:T(1024)(128)(4,1)}), s8[4194304]{0:T(1024)(128)(4,1)S(1)}, s32[]{:S(2)}) async-start(s8[8388608]{0:T(1024)(128)(4,1)} %bitcast.67), calls=%async_computation.3 | async-start | bytes 8388608
  53.7 4.8 %copy-start.2 = (bf16[512,4096]{1,0:T(8,128)(2,1)}, bf16[512,4096]{1,0:T(8,128)(2,1)S(1)}, u32[]{:S(2)}) copy-start(bf16[512,4096]{1,0:T(8,128)(2,1)S(1)} %convolution_convert_fusion) | copy-start | bytes 12582916
  58.5 1.9 %copy-start = (bf16[512,4096]{1,0:T(8,128)(2,1)}, bf16[512,4096]{1,0:T(8,128)(2,1)S(1)}, u32[]{:S(2)}) copy-start(bf16[512,4096]{1,0:T(8,128)(2,1)S(1)} %convolution_convert_fusion.1) | copy-start | bytes 12582916
  60.5 4.5 %copy-start.5 = (bf16[128,4096]{1,0:T(8,128)(2,1)S(1)}, bf16[128,4096]{1,0:T(8,128)(2,1)}, u32[]{:S(2)}) copy-start(bf16[128,4096]{1,0:T(8,128)(2,1)} %param.6) | copy-start | bytes 3145732
  62.8 54.3 %collective-permute-start = (bf16[2,256,4096]{2,1,0:T(8,128)(2,1)}, bf16[2,256,4096]{2,1,0:T(8,128)(2,1)}, u32[]{:S(2)}, u32[]{:S(2)}) collective-permute-start(bf16[2,256,4096]{2,1,0:T(8,128)(2,1)} %pad_maximum_fusion), channel_id=1, source_target_pairs={{0,1},{1,2},{2,3},{3,4},{4,5},{5,6},{6,7},{7,8},{8,9},{9,10},{10,1... | collective-permute-start | bytes 12582920 | tf_op jit(solution)/shard_map/ppermute | solution.py:20
  69.3 3.6 %copy-start.1 = (bf16[512,4096]{1,0:T(8,128)(2,1)S(1)}, bf16[512,4096]{1,0:T(8,128)(2,1)}, u32[]{:S(2)}) copy-start(bf16[512,4096]{1,0:T(8,128)(2,1)} %copy-done) | copy-start | bytes 12582916
  124.9 2.6 %copy-start.3 = (f32[3,32,64,256]{3,2,1,0:T(8,128)}, f32[3,32,64,256]{3,2,1,0:T(8,128)S(1)}, u32[]{:S(2)}) copy-start(f32[3,32,64,256]{3,2,1,0:T(8,128)S(1)} %fusion.1) | copy-start | bytes 18874372
  127.6 2.4 %copy-start.4 = (bf16[1,32,32,8,128]{4,3,1,2,0:T(8,128)(2,1)S(1)}, bf16[1,32,32,8,128]{4,3,1,2,0:T(8,128)(2,1)}, u32[]{:S(2)}) copy-start(bf16[1,32,32,8,128]{4,3,1,2,0:T(8,128)(2,1)} %copy.58) | copy-start | bytes 6291460
where the time goes:
time: 150 us
  waiting for transfers between devices  64.9 us (43%)
  matrix products  30.9 us (21%)
  local copies, waits for them, and re-layouts  28.8 us (19%)
  blocking collectives  9 us (6%)
  other arithmetic  8.69 us (6%)
  starting transfers between devices  7.12 us (5%)
    ppermute x1, waiting for transfers between devices, from_behind(): lax.ppermute(value, axis, [(source, source + steps) for source in range(l...  41.4 us
    all_to_all x1, waiting for transfers between devices, body(): lax.all_to_all(found, 'db', split_axis=0, concat_axis=0, tiled=True)  23.5 us
    dot_general x1, matrix products, body(): jnp.einsum('bhqk,bkhd->bqhd', weights, all_values, preferred_element_type...  15.3 us
    unnamed x23, local copies, waits for them, and re-layouts  12.6 us
    all_to_all x1, blocking collectives, body(): lax.all_to_all(requests, 'db', split_axis=0, concat_axis=0, tiled=True)  9 us
    dot_general x1, matrix products, project(): jnp.dot(flat, value_weight, preferred_element_type=jnp.float32)  8.26 us
    concatenate x2, local copies, waits for them, and re-layouts, body(): jnp.concatenate([prev_values, values], axis=0)  5.45 us
    all_to_all x1, starting transfers between devices, body(): lax.all_to_all(found, 'db', split_axis=0, concat_axis=0, tiled=True)  5.03 us
  transfers between devices with their start and end apart: 2, of which 2 were waited for; matrix products, arithmetic and copies ran while one was open for 7% of the time, Pallas kernels for 0%

commit v1 on v0

v1 whole, which is shorter than its diff:
```python
import functools
import math

import jax
import jax.numpy as jnp
from jax import lax
from jax.experimental import pallas as pl
from jax.experimental.pallas import tpu as pltpu
from jax.sharding import PartitionSpec as P

H = 32
HD = 128
DE = 1024
D = 4096
CL = 64
NB = 2
NT = 128
LENGTH = 2048
BLK_SH = 16
N_DB = 4
PER_SEQ = 16
CHUNKS = (64, 64)
TILE = 1024
MESH = pl.DeviceIdType.MESH


def kernel(
    queries, encoded, key_weight, value_weight, shard, slot, out,
    req, enc, wk, wv, q, q_next, q_rows, keys, values, picks, o_send, o_recv, o_own,
    *rest,
):
    n = len(CHUNKS)
    send = rest[:n]
    recv = rest[n : 2 * n]
    local_sem, req_send, req_recv, blk_send, blk_recv, q_sem, o_sem = rest[2 * n :]
    z = lax.axis_index("db")
    s = lax.axis_index("seq")
    base = (s // PER_SEQ) * PER_SEQ
    place = s % PER_SEQ
    ahead = (z, base + (place + 1) % PER_SEQ)
    behind = (z, base + (place + PER_SEQ - 1) % PER_SEQ)
    column = [((z + step) % N_DB, s) for step in (1, 2, 3)]

    load_enc = pltpu.make_async_copy(encoded, enc, local_sem.at[0])
    load_q = pltpu.make_async_copy(queries, q, local_sem.at[1])
    load_wk = pltpu.make_async_copy(key_weight, wk, local_sem.at[2])
    load_wv = pltpu.make_async_copy(value_weight, wv, local_sem.at[3])
    load_enc.start()
    load_q.start()
    load_wk.start()
    load_wv.start()

    for g in range(2):
        for j in range(NB):
            req[z, g * NB + j] = shard[g, j] * BLK_SH + slot[g, j]

    barrier = pltpu.get_barrier_semaphore()
    for partner in [*column, ahead, behind]:
        pl.semaphore_signal(barrier, inc=1, device_id=partner, device_id_type=MESH)
    pl.semaphore_wait(barrier, 5)

    asks = []
    for i, partner in enumerate(column):
        ask = pltpu.make_async_remote_copy(
            src_ref=req.at[z], dst_ref=req.at[z],
            send_sem=req_send.at[i], recv_sem=req_recv.at[i],
            device_id=partner, device_id_type=MESH,
        )
        ask.start()
        asks.append(ask)

    load_enc.wait()
    for ask in asks:
        ask.wait()

    def wanted(who, g, owner):
        first, second = req[who, g * NB], req[who, g * NB + 1]
        from_second = jnp.where(second // BLK_SH == owner, second % BLK_SH, 0)
        return jnp.where(first // BLK_SH == owner, first % BLK_SH, from_second)

    places = [[wanted((z + step) % N_DB, g, z) for g in range(2)] for step in range(N_DB)]
    blocks = []
    row = 0
    for c, rows in enumerate(CHUNKS):
        moves = []
        for i, partner in enumerate(column):
            for g in range(2):
                send[c][i, g] = enc[places[i + 1][g], row : row + rows, :]
            move = pltpu.make_async_remote_copy(
                src_ref=send[c].at[i], dst_ref=recv[c].at[z],
                send_sem=blk_send.at[c, i], recv_sem=blk_recv.at[c, i],
                device_id=partner, device_id_type=MESH,
            )
            move.start()
            moves.append(move)
        for g in range(2):
            recv[c][z, g] = enc[places[0][g], row : row + rows, :]
        blocks.append(moves)
        row += rows

    load_q.wait()
    give_q = pltpu.make_async_remote_copy(
        src_ref=q.at[pl.ds(0, CL)], dst_ref=q_next,
        send_sem=q_sem.at[0], recv_sem=q_sem.at[1],
        device_id=behind, device_id_type=MESH,
    )
    give_q.start()
    give_q.wait()

    def shift_q(i, carry):
        cols = pl.ds(pl.multiple_of(i * 512, 512), 512)
        both = jnp.concatenate([q[:, cols], q_next[:, cols]], axis=0).astype(jnp.float32)
        q_rows[:, cols] = pltpu.roll(both, 192 - (CL - 1), 0)[: 2 * CL].astype(jnp.bfloat16)
        return carry

    lax.fori_loop(0, D // 512, shift_q, 0)

    load_wk.wait()
    load_wv.wait()
    row = 0
    for c, rows in enumerate(CHUNKS):
        for move in blocks[c]:
            move.wait()
        for g in range(2):
            for j in range(NB):
                at = (g * NB + j) * rows
                picks[at : at + rows, :] = recv[c][shard[g, j], g]
        for weight, held in ((wk, keys), (wv, values)):

            def project(i, carry, weight=weight, held=held, row=row, rows=rows):
                cols = pl.ds(pl.multiple_of(i * TILE, TILE), TILE)
                done = jnp.dot(
                    picks[0 : 4 * rows, :], weight[:, cols], preferred_element_type=jnp.float32
                ).astype(jnp.bfloat16)
                for g in range(2):
                    held[g, NB * row : NB * (row + rows), cols] = done[g * NB * rows : (g + 1) * NB * rows]
                return carry

            lax.fori_loop(0, D // TILE, project, 0)
        row += rows

    def attend(g, into):
        def head(i, carry):
            for u in range(4):
                cols = pl.ds(pl.multiple_of((i * 4 + u) * HD, HD), HD)
                scores = lax.dot_general(
                    q_rows[g * CL : (g + 1) * CL, cols], keys[g, :, cols],
                    (((1,), (1,)), ((), ())), preferred_element_type=jnp.float32,
                ) * (1.0 / math.sqrt(HD))
                top = jnp.max(scores, axis=1, keepdims=True)
                raised = jnp.exp(scores - top)
                total = jnp.sum(raised, axis=1, keepdims=True)
                weights = (raised / total).astype(jnp.bfloat16)
                into[:, cols] = jnp.dot(
                    weights, values[g, :, cols], preferred_element_type=jnp.float32
                ).astype(jnp.bfloat16)
            return carry

        lax.fori_loop(0, H // 4, head, 0)

    attend(1, o_send)
    give_o = pltpu.make_async_remote_copy(
        src_ref=o_send, dst_ref=o_recv,
        send_sem=o_sem.at[0], recv_sem=o_sem.at[1],
        device_id=ahead, device_id_type=MESH,
    )
    give_o.start()
    attend(0, o_own)
    give_o.wait()

    opening = place == 0

    def finish(i, carry):
        cols = pl.ds(pl.multiple_of(i * 512, 512), 512)
        both = jnp.concatenate(
            [o_recv[:, cols], o_own[:, cols], o_send[0:16, cols]], axis=0
        ).astype(jnp.float32)
        moved = pltpu.roll(both, 2 * CL + 15, 0)[: 2 * CL]
        token = lax.broadcasted_iota(jnp.int32, (2 * CL, 512), 0)
        blank = jnp.logical_and(opening, token < CL - 1)
        out[:, cols] = jnp.where(blank, 0.0, moved).astype(jnp.bfloat16)
        return carry

    lax.fori_loop(0, D // 512, finish, 0)


def body(queries, encoded, key_weight, value_weight, nbr_shard, nbr_slot):
    n = len(CHUNKS)
    any_spec = pl.BlockSpec(memory_space=pl.ANY)
    smem = pl.BlockSpec(memory_space=pltpu.SMEM)
    bf16 = jnp.bfloat16
    return pl.pallas_call(
        kernel,
        out_shape=jax.ShapeDtypeStruct((2 * CL, D), bf16),
        in_specs=[any_spec] * 4 + [smem] * 2,
        out_specs=pl.BlockSpec(memory_space=pltpu.VMEM),
        scratch_shapes=[
            pltpu.SMEM((N_DB, 4), jnp.int32),
            pltpu.VMEM((BLK_SH, NT, DE), bf16),
            pltpu.VMEM((DE, D), bf16),
            pltpu.VMEM((DE, D), bf16),
            pltpu.VMEM((2 * CL, D), bf16),
            pltpu.VMEM((CL, D), bf16),
            pltpu.VMEM((2 * CL, D), bf16),
            pltpu.VMEM((2, NB * NT, D), bf16),
            pltpu.VMEM((2, NB * NT, D), bf16),
            pltpu.VMEM((4 * max(CHUNKS), DE), bf16),
            pltpu.VMEM((CL, D), bf16),
            pltpu.VMEM((CL, D), bf16),
            pltpu.VMEM((CL, D), bf16),
            *[pltpu.VMEM((3, 2, rows, DE), bf16) for rows in CHUNKS],
            *[pltpu.VMEM((N_DB, 2, rows, DE), bf16) for rows in CHUNKS],
            pltpu.SemaphoreType.DMA((4,)),
            pltpu.SemaphoreType.DMA((3,)),
            pltpu.SemaphoreType.DMA((3,)),
            pltpu.SemaphoreType.DMA((n, 3)),
            pltpu.SemaphoreType.DMA((n, 3)),
            pltpu.SemaphoreType.DMA((2,)),
            pltpu.SemaphoreType.DMA((2,)),
        ],
        compiler_params=pltpu.CompilerParams(
            collective_id=0, has_side_effects=True, vmem_limit_bytes=58 << 20
        ),
        name="retro",
    )(queries, encoded, key_weight, value_weight, nbr_shard, nbr_slot)


def solution(mesh):
    placed = (
        P(("db", "seq"), None),
        P("db", None, None),
        P(),
        P(),
        P(("db", "seq"), None),
        P(("db", "seq"), None),
    )
    return jax.shard_map(
        body, mesh=mesh, in_specs=placed, out_specs=P(("db", "seq"), None), check_vma=False
    )
```

time: 150 us -> 64.2 us (0.43)
  the two profiles are of different devices: /device:TPU:32 before, /device:TPU:0 now
where the time goes in v1:
time: 64.2 us; the launch traced here: 64 us
  Pallas kernels  61.7 us (96%)
  local copies, waits for them, and re-layouts  2.29 us (4%)
    pallas_call x1, Pallas kernels, body(): pl.pallas_call(kernel, out_shape=jax.ShapeDtypeStruct((2 * CL, D), bf16),...  61.7 us
    unnamed x1, local copies, waits for them, and re-layouts  2.29 us

profile of v1, /device:TPU:0, one launch (start us, length us, event | category | flops | bytes accessed | tf_op | source)
XLA Modules:
  0.0 64.0 jit_solution(17776320023146922802)
XLA Ops:
  0.0 61.7 %retro.1 = bf16[128,4096]{1,0:T(8,128)(2,1)} custom-call(bf16[128,4096]{1,0:T(8,128)(2,1)} %queries.1, bf16[16,128,1024]{2,1,0:T(8,128)(2,1)} %encoded.1, bf16[1024,4096]{1,0:T(8,128)(2,1)} %key_weight.1, bf16[1024,4096]{1,0:T(8,128)(2,1)} %value_weight.1, s32[2,2]{1,0:T(2,128)} %shard.1, s32[2,2]{1,0:T(2,128)} %slot.1), custom_call_target="tpu_custom_call" | custom-call | tf_op jit(solution)/shard_map/retro/pallas_call | solution.py:192
  61.7 2.3 %copy.8 = bf16[128,4096]{1,0:T(8,128)(2,1)} copy(bf16[128,4096]{1,0:T(8,128)(2,1)} %retro.1) | data formatting | bytes 2097152

commit v2 on v1

v2 whole, which is shorter than its diff:
```python
import functools
import math

import jax
import jax.numpy as jnp
from jax import lax
from jax.experimental import pallas as pl
from jax.experimental.pallas import tpu as pltpu
from jax.sharding import PartitionSpec as P

H = 32
HD = 128
DE = 1024
D = 4096
CL = 64
NB = 2
NT = 128
LENGTH = 2048
BLK_SH = 16
N_DB = 4
PER_SEQ = 16
CHUNKS = (32, 32, 32, 32)
TILE = 2048
HEADS = 16
SCALE = math.log2(math.e) / math.sqrt(HD)
MESH = pl.DeviceIdType.MESH


def kernel(
    queries, encoded, key_weight, value_weight, shard, slot, out,
    mine, req, enc, wk, wv, q, q_prev, q_rows, keys, values, picks, row_send, row_recv,
    *rest,
):
    n = len(CHUNKS)
    send = rest[:n]
    recv = rest[n : 2 * n]
    local_sem, req_send, req_recv, blk_send, blk_recv, q_sem, row_sem = rest[2 * n :]
    z = lax.axis_index("db")
    s = lax.axis_index("seq")
    base = (s // PER_SEQ) * PER_SEQ
    place = s % PER_SEQ
    ahead = base + (place + 1) % PER_SEQ
    behind = base + (place + PER_SEQ - 1) % PER_SEQ

    load_enc = pltpu.make_async_copy(encoded, enc, local_sem.at[0])
    load_q = pltpu.make_async_copy(queries, q, local_sem.at[1])
    load_wk = pltpu.make_async_copy(key_weight, wk, local_sem.at[2])
    load_wv = pltpu.make_async_copy(value_weight, wv, local_sem.at[3])
    load_enc.start()
    load_q.start()
    load_wk.start()
    load_wv.start()

    for g in range(2):
        for j in range(NB):
            wanted = shard[g, j] * BLK_SH + slot[g, j]
            mine[1 - g, j] = wanted
            if g == 0:
                req[z, 1, j] = wanted

    barrier = pltpu.get_barrier_semaphore()

    def tell(where):
        pl.semaphore_signal(barrier, inc=1, device_id=where, device_id_type=MESH)

    tell((z, ahead))
    for step in range(N_DB):
        tell(((z + step) % N_DB, behind))
        if step:
            tell(((z + step) % N_DB, s))
    pl.semaphore_wait(barrier, 2 * N_DB)

    asks = []
    for step in range(N_DB):
        for g in range(2):
            if g == 1 and step == 0:
                continue
            ask = pltpu.make_async_remote_copy(
                src_ref=mine.at[g], dst_ref=req.at[z, g],
                send_sem=req_send.at[g, step], recv_sem=req_recv.at[g, step],
                device_id=((z + step) % N_DB, ahead if g == 0 else s), device_id_type=MESH,
            )
            ask.start()
            asks.append(ask)
    give_q = pltpu.make_async_remote_copy(
        src_ref=queries.at[pl.ds(2 * CL - 16, 16)], dst_ref=q_prev,
        send_sem=q_sem.at[0], recv_sem=q_sem.at[1],
        device_id=(z, ahead), device_id_type=MESH,
    )
    give_q.start()

    load_enc.wait()
    for ask in asks:
        ask.wait()

    def place_in(who, g):
        first, second = req[who, g, 0], req[who, g, 1]
        from_second = jnp.where(second // BLK_SH == z, second % BLK_SH, 0)
        return jnp.where(first // BLK_SH == z, first % BLK_SH, from_second)

    places = [[place_in((z + step) % N_DB, g) for g in range(2)] for step in range(N_DB)]
    owners = [[req[z, g, j] // BLK_SH for j in range(NB)] for g in range(2)]
    blocks = []
    row = 0
    for c, rows in enumerate(CHUNKS):
        moves = []
        for i in range(3):
            for g in range(2):
                send[c][i, g] = enc[places[i + 1][g], row : row + rows, :]
            move = pltpu.make_async_remote_copy(
                src_ref=send[c].at[i], dst_ref=recv[c].at[z],
                send_sem=blk_send.at[c, i], recv_sem=blk_recv.at[c, i],
                device_id=((z + i + 1) % N_DB, s), device_id_type=MESH,
            )
            move.start()
            moves.append(move)
        for g in range(2):
            recv[c][z, g] = enc[places[0][g], row : row + rows, :]
        blocks.append(moves)
        row += rows

    load_q.wait()
    give_q.wait()

    def shift_q(i, carry):
        cols = pl.ds(pl.multiple_of(i * 512, 512), 512)
        both = jnp.concatenate([q_prev[:, cols], q[:, cols]], axis=0).astype(jnp.float32)
        q_rows[:, cols] = pltpu.roll(both, 2 * CL + 1, 0)[: 2 * CL].astype(jnp.bfloat16)
        return carry

    lax.fori_loop(0, D // 512, shift_q, 0)

    load_wk.wait()
    load_wv.wait()
    row = 0
    for c, rows in enumerate(CHUNKS):
        for move in blocks[c]:
            move.wait()
        for g in range(2):
            for j in range(NB):
                at = (g * NB + j) * rows
                picks[at : at + rows, :] = recv[c][owners[g][j], g]
        for weight, held in ((wk, keys), (wv, values)):

            def project(i, carry, weight=weight, held=held, row=row, rows=rows):
                cols = pl.ds(pl.multiple_of(i * TILE, TILE), TILE)
                done = jnp.dot(
                    picks[0 : 4 * rows, :], weight[:, cols], preferred_element_type=jnp.float32
                ).astype(jnp.bfloat16)
                for g in range(2):
                    held[g, NB * row : NB * (row + rows), cols] = done[g * NB * rows : (g + 1) * NB * rows]
                return carry

            lax.fori_loop(0, D // TILE, project, 0)
        row += rows

    def attend(g, half):
        heads = [pl.ds((half * HEADS + u) * HD, HD) for u in range(HEADS)]
        scores = [
            lax.dot_general(
                q_rows[g * CL : (g + 1) * CL, cols], keys[g, :, cols],
                (((1,), (1,)), ((), ())), preferred_element_type=jnp.float32,
            )
            for cols in heads
        ]
        tops = [jnp.max(score, axis=1, keepdims=True) for score in scores]
        raised = [jnp.exp2((score - top) * SCALE) for score, top in zip(scores, tops)]
        totals = [jnp.sum(each, axis=1, keepdims=True) for each in raised]
        weights = [
            (each * (1.0 / total)).astype(jnp.bfloat16) for each, total in zip(raised, totals)
        ]
        mixed = [
            jnp.dot(weight, values[g, :, cols], preferred_element_type=jnp.float32)
            for weight, cols in zip(weights, heads)
        ]
        return list(zip(heads, mixed))

    for half in range(H // HEADS):
        done = attend(0, half)
        for cols, each in done:
            moved = jnp.where(place == 0, 0.0, pltpu.roll(each, CL - 1, 0))
            out[0:CL, cols] = moved.astype(jnp.bfloat16)
        row_send[half * HEADS : (half + 1) * HEADS, :] = jnp.concatenate(
            [each[0:1] for _, each in done], axis=0
        ).astype(jnp.bfloat16)
    give_row = pltpu.make_async_remote_copy(
        src_ref=row_send, dst_ref=row_recv,
        send_sem=row_sem.at[0], recv_sem=row_sem.at[1],
        device_id=(z, behind), device_id_type=MESH,
    )
    give_row.start()
    for half in range(H // HEADS):
        for cols, each in attend(1, half):
            out[CL : 2 * CL, cols] = pltpu.roll(each, CL - 1, 0).astype(jnp.bfloat16)
            out[CL - 1 : CL, cols] = each[0:1].astype(jnp.bfloat16)
    give_row.wait()
    last = row_recv[...]
    for h in range(H):
        out[2 * CL - 1 : 2 * CL, h * HD : (h + 1) * HD] = last[h : h + 1]


def body(queries, encoded, key_weight, value_weight, nbr_shard, nbr_slot):
    n = len(CHUNKS)
    any_spec = pl.BlockSpec(memory_space=pl.ANY)
    smem = pl.BlockSpec(memory_space=pltpu.SMEM)
    bf16 = jnp.bfloat16
    return pl.pallas_call(
        kernel,
        out_shape=jax.ShapeDtypeStruct((2 * CL, D), bf16),
        in_specs=[any_spec] * 4 + [smem] * 2,
        out_specs=pl.BlockSpec(memory_space=pltpu.VMEM),
        scratch_shapes=[
            pltpu.SMEM((2, NB), jnp.int32),
            pltpu.SMEM((N_DB, 2, NB), jnp.int32),
            pltpu.VMEM((BLK_SH, NT, DE), bf16),
            pltpu.VMEM((DE, D), bf16),
            pltpu.VMEM((DE, D), bf16),
            pltpu.VMEM((2 * CL, D), bf16),
            pltpu.VMEM((16, D), bf16),
            pltpu.VMEM((2 * CL, D), bf16),
            pltpu.VMEM((2, NB * NT, D), bf16),
            pltpu.VMEM((2, NB * NT, D), bf16),
            pltpu.VMEM((4 * max(CHUNKS), DE), bf16),
            pltpu.VMEM((H, HD), bf16),
            pltpu.VMEM((H, HD), bf16),
            *[pltpu.VMEM((3, 2, rows, DE), bf16) for rows in CHUNKS],
            *[pltpu.VMEM((N_DB, 2, rows, DE), bf16) for rows in CHUNKS],
            pltpu.SemaphoreType.DMA((4,)),
            pltpu.SemaphoreType.DMA((2, N_DB)),
            pltpu.SemaphoreType.DMA((2, N_DB)),
            pltpu.SemaphoreType.DMA((n, 3)),
            pltpu.SemaphoreType.DMA((n, 3)),
            pltpu.SemaphoreType.DMA((2,)),
            pltpu.SemaphoreType.DMA((2,)),
        ],
        compiler_params=pltpu.CompilerParams(
            collective_id=0, has_side_effects=True, vmem_limit_bytes=58 << 20
        ),
        name="retro",
    )(queries, encoded, key_weight, value_weight, nbr_shard, nbr_slot)


def solution(mesh):
    placed = (
        P(("db", "seq"), None),
        P("db", None, None),
        P(),
        P(),
        P(("db", "seq"), None),
        P(("db", "seq"), None),
    )
    return jax.shard_map(
        body, mesh=mesh, in_specs=placed, out_specs=P(("db", "seq"), None), check_vma=False
    )
```

time: 64.2 us -> 45.8 us (0.71)
  the two profiles are of different devices: /device:TPU:0 before, /device:TPU:1 now
where the time goes in v2:
time: 45.8 us; the launch traced here: 45.7 us
  Pallas kernels  43.4 us (95%)
  local copies, waits for them, and re-layouts  2.29 us (5%)
    pallas_call x1, Pallas kernels, body(): pl.pallas_call(kernel, out_shape=jax.ShapeDtypeStruct((2 * CL, D), bf16),...  43.4 us
    unnamed x1, local copies, waits for them, and re-layouts  2.29 us

profile of v2, /device:TPU:1, one launch (start us, length us, event | category | flops | bytes accessed | tf_op | source)
XLA Modules:
  0.0 45.7 jit_solution(16689238491099998790)
XLA Ops:
  0.0 43.4 %retro.1 = bf16[128,4096]{1,0:T(8,128)(2,1)} custom-call(bf16[128,4096]{1,0:T(8,128)(2,1)} %queries.1, bf16[16,128,1024]{2,1,0:T(8,128)(2,1)} %encoded.1, bf16[1024,4096]{1,0:T(8,128)(2,1)} %key_weight.1, bf16[1024,4096]{1,0:T(8,128)(2,1)} %value_weight.1, s32[2,2]{1,0:T(2,128)} %shard.1, s32[2,2]{1,0:T(2,128)} %slot.1), custom_call_target="tpu_custom_call" | custom-call | tf_op jit(solution)/shard_map/retro/pallas_call | solution.py:207
  43.4 2.3 %copy.8 = bf16[128,4096]{1,0:T(8,128)(2,1)} copy(bf16[128,4096]{1,0:T(8,128)(2,1)} %retro.1) | data formatting | bytes 2097152

commit v3 on v2

--- a/solution.py
+++ b/solution.py
@@ -18,6 +18,7 @@
 LENGTH = 2048
 BLK_SH = 16
 N_DB = 4
+SIDE = 4
 PER_SEQ = 16
 CHUNKS = (32, 32, 32, 32)
 TILE = 2048
@@ -34,13 +35,31 @@
     n = len(CHUNKS)
     send = rest[:n]
     recv = rest[n : 2 * n]
-    local_sem, req_send, req_recv, blk_send, blk_recv, q_sem, row_sem = rest[2 * n :]
+    far = rest[2 * n : 3 * n]
+    (
+        local_sem, req_send, req_recv, blk_send, blk_recv, far_send, far_recv, q_sem, row_sem,
+    ) = rest[3 * n :]
     z = lax.axis_index("db")
     s = lax.axis_index("seq")
     base = (s // PER_SEQ) * PER_SEQ
     place = s % PER_SEQ
     ahead = base + (place + 1) % PER_SEQ
     behind = base + (place + PER_SEQ - 1) % PER_SEQ
+    block, core = s // 2, s % 2
+    u = jnp.where(core == 0, block // SIDE, block % SIDE)
+    v = jnp.where(core == 0, block % SIDE, block // SIDE)
+    spot = u * SIDE + v
+
+    def chip(u_of, v_of):
+        x = jnp.where(core == 0, u_of, v_of)
+        y = jnp.where(core == 0, v_of, u_of)
+        return (z, (x * SIDE + y) * 2 + core)
+
+    opposite = ((z + 2) % N_DB, s)
+    other_core = (z, block * 2 + 1 - core)
+    along_v = [chip(u, (v + step) % SIDE) for step in (1, 3, 2)]
+    along_u = [chip((u + step) % SIDE, v) for step in (1, 3, 2)]
+    near = [((z + step) % N_DB, s) for step in (1, 3)]
 
     load_enc = pltpu.make_async_copy(encoded, enc, local_sem.at[0])
     load_q = pltpu.make_async_copy(queries, q, local_sem.at[1])
@@ -64,20 +83,33 @@
         pl.semaphore_signal(barrier, inc=1, device_id=where, device_id_type=MESH)
 
     tell((z, ahead))
-    for step in range(N_DB):
+    for step in (0, 1, 3):
         tell(((z + step) % N_DB, behind))
-        if step:
-            tell(((z + step) % N_DB, s))
-    pl.semaphore_wait(barrier, 2 * N_DB)
+    for partner in [*near, opposite, *along_v, *along_u, other_core]:
+        tell(partner)
+    pl.semaphore_wait(barrier, 14)
+
+    brings = []
+    row = 0
+    for c, rows in enumerate(CHUNKS):
+        half = rows // 2
+        bring = pltpu.make_async_remote_copy(
+            src_ref=encoded.at[block, pl.ds(row + core * half, half)], dst_ref=far[c].at[core, spot],
+            send_sem=far_send.at[c, 0], recv_sem=far_recv.at[c, 0],
+            device_id=opposite, device_id_type=MESH,
+        )
+        bring.start()
+        brings.append(bring)
+        row += rows
 
     asks = []
-    for step in range(N_DB):
+    for i, step in enumerate((0, 1, 3)):
         for g in range(2):
             if g == 1 and step == 0:
                 continue
             ask = pltpu.make_async_remote_copy(
                 src_ref=mine.at[g], dst_ref=req.at[z, g],
-                send_sem=req_send.at[g, step], recv_sem=req_recv.at[g, step],
+                send_sem=req_send.at[g, i], recv_sem=req_recv.at[g, i],
                 device_id=((z + step) % N_DB, ahead if g == 0 else s), device_id_type=MESH,
             )
             ask.start()
@@ -89,28 +121,56 @@
     )
     give_q.start()
 
+    def spread(c, first, partners, source):
+        moves = []
+        for i, partner in enumerate(partners):
+            move = pltpu.make_async_remote_copy(
+                src_ref=source, dst_ref=source,
+                send_sem=far_send.at[c, first + i], recv_sem=far_recv.at[c, first + i],
+                device_id=partner, device_id_type=MESH,
+            )
+            move.start()
+            moves.append(move)
+        return moves
+
+    def pieces(c):
+        brings[c].wait()
+        return spread(c, 1, along_v, far[c].at[core, spot])
+
+    def bundles(c, moves):
+        for move in moves:
+            move.wait()
+        return spread(c, 4, along_u, far[c].at[core, pl.ds(u * SIDE, SIDE)])
+
+    def share(c, moves):
+        for move in moves:
+            move.wait()
+        return spread(c, 7, [other_core], far[c].at[core])
+
+    ones = [pieces(0)]
     load_enc.wait()
     for ask in asks:
         ask.wait()
 
-    def place_in(who, g):
+    def place_in(who, g, owner):
         first, second = req[who, g, 0], req[who, g, 1]
-        from_second = jnp.where(second // BLK_SH == z, second % BLK_SH, 0)
-        return jnp.where(first // BLK_SH == z, first % BLK_SH, from_second)
-
-    places = [[place_in((z + step) % N_DB, g) for g in range(2)] for step in range(N_DB)]
+        from_second = jnp.where(second // BLK_SH == owner, second % BLK_SH, 0)
+        return jnp.where(first // BLK_SH == owner, first % BLK_SH, from_second)
+
+    places = [[place_in((z + step) % N_DB, g, z) for g in range(2)] for step in (0, 1, 3)]
+    far_places = [place_in(z, g, (z + 2) % N_DB) for g in range(2)]
     owners = [[req[z, g, j] // BLK_SH for j in range(NB)] for g in range(2)]
     blocks = []
     row = 0
     for c, rows in enumerate(CHUNKS):
         moves = []
-        for i in range(3):
+        for i, partner in enumerate(near):
             for g in range(2):
                 send[c][i, g] = enc[places[i + 1][g], row : row + rows, :]
             move = pltpu.make_async_remote_copy(
                 src_ref=send[c].at[i], dst_ref=recv[c].at[z],
                 send_sem=blk_send.at[c, i], recv_sem=blk_recv.at[c, i],
-                device_id=((z + i + 1) % N_DB, s), device_id_type=MESH,
+                device_id=partner, device_id_type=MESH,
             )
             move.start()
             moves.append(move)
@@ -119,6 +179,12 @@
         blocks.append(moves)
         row += rows
 
+    twos = []
+    for c in range(1, n):
+        ones.append(pieces(c))
+        twos.append(bundles(c - 1, ones[c - 1]))
+    twos.append(bundles(n - 1, ones[n - 1]))
+
     load_q.wait()
     give_q.wait()
 
@@ -130,12 +196,18 @@
 
     lax.fori_loop(0, D // 512, shift_q, 0)
 
+    shares = [share(0, twos[0])]
     load_wk.wait()
     load_wv.wait()
     row = 0
     for c, rows in enumerate(CHUNKS):
-        for move in blocks[c]:
+        half = rows // 2
+        for move in [*blocks[c], *shares[c]]:
             move.wait()
+        for g in range(2):
+            at = far_places[g]
+            recv[c][(z + 2) % N_DB, g, 0:half] = far[c][0, at]
+            recv[c][(z + 2) % N_DB, g, half:rows] = far[c][1, at % SIDE * SIDE + at // SIDE]
         for g in range(2):
             for j in range(NB):
                 at = (g * NB + j) * rows
@@ -152,6 +224,8 @@
                 return carry
 
             lax.fori_loop(0, D // TILE, project, 0)
+            if weight is wk and c + 1 < n:
+                shares.append(share(c + 1, twos[c + 1]))
         row += rows
 
     def attend(g, half):
@@ -223,13 +297,16 @@
             pltpu.VMEM((4 * max(CHUNKS), DE), bf16),
             pltpu.VMEM((H, HD), bf16),
             pltpu.VMEM((H, HD), bf16),
-            *[pltpu.VMEM((3, 2, rows, DE), bf16) for rows in CHUNKS],
+            *[pltpu.VMEM((2, 2, rows, DE), bf16) for rows in CHUNKS],
             *[pltpu.VMEM((N_DB, 2, rows, DE), bf16) for rows in CHUNKS],
+            *[pltpu.VMEM((2, BLK_SH, rows // 2, DE), bf16) for rows in CHUNKS],
             pltpu.SemaphoreType.DMA((4,)),
-            pltpu.SemaphoreType.DMA((2, N_DB)),
-            pltpu.SemaphoreType.DMA((2, N_DB)),
-            pltpu.SemaphoreType.DMA((n, 3)),
-            pltpu.SemaphoreType.DMA((n, 3)),
+            pltpu.SemaphoreType.DMA((2, 3)),
+            pltpu.SemaphoreType.DMA((2, 3)),
+            pltpu.SemaphoreType.DMA((n, 2)),
+            pltpu.SemaphoreType.DMA((n, 2)),
+            pltpu.SemaphoreType.DMA((n, 8)),
+            pltpu.SemaphoreType.DMA((n, 8)),
             pltpu.SemaphoreType.DMA((2,)),
             pltpu.SemaphoreType.DMA((2,)),
         ],

time: 45.8 us -> 44.8 us (0.978)
  Pallas kernels: 43.4 us -> 42.4 us
    pallas_call x1, Pallas kernels: 43.4 us -> 42.4 us  [body(): pl.pallas_call(kernel, out_shape=jax.ShapeDtypeStruct((2 * CL, D), bf16),...]
where the time goes in v3:
time: 44.8 us; the launch traced here: 44.7 us
  Pallas kernels  42.4 us (95%)
  local copies, waits for them, and re-layouts  2.29 us (5%)
    pallas_call x1, Pallas kernels, body(): pl.pallas_call(kernel, out_shape=jax.ShapeDtypeStruct((2 * CL, D), bf16),...  42.4 us
    unnamed x1, local copies, waits for them, and re-layouts  2.29 us

profile of v3, /device:TPU:1, one launch (start us, length us, event | category | flops | bytes accessed | tf_op | source)
XLA Modules:
  0.0 44.7 jit_solution(2648486805590922951)
XLA Ops:
  0.0 42.4 %retro.1 = bf16[128,4096]{1,0:T(8,128)(2,1)} custom-call(bf16[128,4096]{1,0:T(8,128)(2,1)} %queries.1, bf16[16,128,1024]{2,1,0:T(8,128)(2,1)} %encoded.1, bf16[1024,4096]{1,0:T(8,128)(2,1)} %key_weight.1, bf16[1024,4096]{1,0:T(8,128)(2,1)} %value_weight.1, s32[2,2]{1,0:T(2,128)} %shard.1, s32[2,2]{1,0:T(2,128)} %slot.1), custom_call_target="tpu_custom_call" | custom-call | tf_op jit(solution)/shard_map/retro/pallas_call | solution.py:281
  42.4 2.3 %copy.8 = bf16[128,4096]{1,0:T(8,128)(2,1)} copy(bf16[128,4096]{1,0:T(8,128)(2,1)} %retro.1) | data formatting | bytes 2097152

commit v4 on v3

--- a/solution.py
+++ b/solution.py
@@ -21,7 +21,9 @@
 SIDE = 4
 PER_SEQ = 16
 CHUNKS = (32, 32, 32, 32)
-TILE = 2048
+DIRECT = 1
+PLAN = {(0, False): (1,), (1, False): (2,), (2, False): (3,)}
+TILE = 4096
 HEADS = 16
 SCALE = math.log2(math.e) / math.sqrt(HD)
 MESH = pl.DeviceIdType.MESH
@@ -67,8 +69,6 @@
     load_wv = pltpu.make_async_copy(value_weight, wv, local_sem.at[3])
     load_enc.start()
     load_q.start()
-    load_wk.start()
-    load_wv.start()
 
     for g in range(2):
         for j in range(NB):
@@ -83,15 +83,16 @@
         pl.semaphore_signal(barrier, inc=1, device_id=where, device_id_type=MESH)
 
     tell((z, ahead))
-    for step in (0, 1, 3):
+    for step in range(N_DB):
         tell(((z + step) % N_DB, behind))
     for partner in [*near, opposite, *along_v, *along_u, other_core]:
         tell(partner)
-    pl.semaphore_wait(barrier, 14)
-
-    brings = []
-    row = 0
-    for c, rows in enumerate(CHUNKS):
+    pl.semaphore_wait(barrier, 15)
+
+    brings = [None] * DIRECT
+    row = sum(CHUNKS[:DIRECT])
+    for c in range(DIRECT, n):
+        rows = CHUNKS[c]
         half = rows // 2
         bring = pltpu.make_async_remote_copy(
             src_ref=encoded.at[block, pl.ds(row + core * half, half)], dst_ref=far[c].at[core, spot],
@@ -103,7 +104,7 @@
         row += rows
 
     asks = []
-    for i, step in enumerate((0, 1, 3)):
+    for i, step in enumerate((0, 1, 3, 2)):
         for g in range(2):
             if g == 1 and step == 0:
                 continue
@@ -121,9 +122,9 @@
     )
     give_q.start()
 
-    def spread(c, first, partners, source):
+    def spread(c, first, pairs):
         moves = []
-        for i, partner in enumerate(partners):
+        for i, (partner, source) in enumerate(pairs):
             move = pltpu.make_async_remote_copy(
                 src_ref=source, dst_ref=source,
                 send_sem=far_send.at[c, first + i], recv_sem=far_recv.at[c, first + i],
@@ -133,22 +134,26 @@
             moves.append(move)
         return moves
 
+    def wait_all(moves):
+        for move in moves:
+            move.wait()
+
     def pieces(c):
         brings[c].wait()
-        return spread(c, 1, along_v, far[c].at[core, spot])
+        return spread(c, 1, [(partner, far[c].at[core, spot]) for partner in along_v])
 
     def bundles(c, moves):
-        for move in moves:
-            move.wait()
-        return spread(c, 4, along_u, far[c].at[core, pl.ds(u * SIDE, SIDE)])
+        wait_all(moves)
+        held = far[c].at[core, pl.ds(u * SIDE, SIDE)]
+        return spread(c, 4, [(partner, held) for partner in along_u])
 
     def share(c, moves):
-        for move in moves:
-            move.wait()
-        return spread(c, 7, [other_core], far[c].at[core])
-
-    ones = [pieces(0)]
+        wait_all(moves)
+        return spread(c, 7, [(other_core, far[c].at[core])])
+
     load_enc.wait()
+    load_wk.start()
+    load_wv.start()
     for ask in asks:
         ask.wait()
 
@@ -157,14 +162,14 @@
         from_second = jnp.where(second // BLK_SH == owner, second % BLK_SH, 0)
         return jnp.where(first // BLK_SH == owner, first % BLK_SH, from_second)
 
-    places = [[place_in((z + step) % N_DB, g, z) for g in range(2)] for step in (0, 1, 3)]
+    places = [[place_in((z + step) % N_DB, g, z) for g in range(2)] for step in (0, 1, 3, 2)]
     far_places = [place_in(z, g, (z + 2) % N_DB) for g in range(2)]
     owners = [[req[z, g, j] // BLK_SH for j in range(NB)] for g in range(2)]
     blocks = []
     row = 0
     for c, rows in enumerate(CHUNKS):
         moves = []
-        for i, partner in enumerate(near):
+        for i, partner in enumerate([*near, opposite] if c < DIRECT else near):
             for g in range(2):
                 send[c][i, g] = enc[places[i + 1][g], row : row + rows, :]
             move = pltpu.make_async_remote_copy(
@@ -179,11 +184,8 @@
         blocks.append(moves)
         row += rows
 
-    twos = []
-    for c in range(1, n):
-        ones.append(pieces(c))
-        twos.append(bundles(c - 1, ones[c - 1]))
-    twos.append(bundles(n - 1, ones[n - 1]))
+    ones = [None] * DIRECT + [pieces(c) for c in range(DIRECT, n)]
+    twos = [None] * DIRECT + [bundles(c, ones[c]) for c in range(DIRECT, n)]
 
     load_q.wait()
     give_q.wait()
@@ -196,7 +198,13 @@
 
     lax.fori_loop(0, D // 512, shift_q, 0)
 
-    shares = [share(0, twos[0])]
+    shares = [[]] * n
+
+    def advance(after):
+        for c in PLAN.get(after, ()):
+            shares[c] = share(c, twos[c])
+
+    advance((-1, True))
     load_wk.wait()
     load_wv.wait()
     row = 0
@@ -204,7 +212,7 @@
         half = rows // 2
         for move in [*blocks[c], *shares[c]]:
             move.wait()
-        for g in range(2):
+        for g in range(2 if c >= DIRECT else 0):
             at = far_places[g]
             recv[c][(z + 2) % N_DB, g, 0:half] = far[c][0, at]
             recv[c][(z + 2) % N_DB, g, half:rows] = far[c][1, at % SIDE * SIDE + at // SIDE]
@@ -224,8 +232,7 @@
                 return carry
 
             lax.fori_loop(0, D // TILE, project, 0)
-            if weight is wk and c + 1 < n:
-                shares.append(share(c + 1, twos[c + 1]))
+            advance((c, weight is wv))
         row += rows
 
     def attend(g, half):
@@ -280,7 +287,7 @@
     bf16 = jnp.bfloat16
     return pl.pallas_call(
         kernel,
-        out_shape=jax.ShapeDtypeStruct((2 * CL, D), bf16),
+        out_shape=pltpu.VMEM((2 * CL, D), bf16),
         in_specs=[any_spec] * 4 + [smem] * 2,
         out_specs=pl.BlockSpec(memory_space=pltpu.VMEM),
         scratch_shapes=[
@@ -297,14 +304,14 @@
             pltpu.VMEM((4 * max(CHUNKS), DE), bf16),
             pltpu.VMEM((H, HD), bf16),
             pltpu.VMEM((H, HD), bf16),
-            *[pltpu.VMEM((2, 2, rows, DE), bf16) for rows in CHUNKS],
+            *[pltpu.VMEM((3, 2, rows, DE), bf16) for rows in CHUNKS],
             *[pltpu.VMEM((N_DB, 2, rows, DE), bf16) for rows in CHUNKS],
             *[pltpu.VMEM((2, BLK_SH, rows // 2, DE), bf16) for rows in CHUNKS],
             pltpu.SemaphoreType.DMA((4,)),
-            pltpu.SemaphoreType.DMA((2, 3)),
-            pltpu.SemaphoreType.DMA((2, 3)),
-            pltpu.SemaphoreType.DMA((n, 2)),
-            pltpu.SemaphoreType.DMA((n, 2)),
+            pltpu.SemaphoreType.DMA((2, N_DB)),
+            pltpu.SemaphoreType.DMA((2, N_DB)),
+            pltpu.SemaphoreType.DMA((n, 3)),
+            pltpu.SemaphoreType.DMA((n, 3)),
             pltpu.SemaphoreType.DMA((n, 8)),
             pltpu.SemaphoreType.DMA((n, 8)),
             pltpu.SemaphoreType.DMA((2,)),

time: 44.8 us -> 40 us (0.89)
  Pallas kernels: 42.4 us -> 38.9 us
  local copies, waits for them, and re-layouts: 2.29 us -> 0.97 us
    pallas_call x1, Pallas kernels: 42.4 us -> 38.9 us  [body(): pl.pallas_call(kernel, out_shape=pltpu.VMEM((2 * CL, D), bf16), in_specs=...]
    unnamed x1, local copies, waits for them, and re-layouts: 2.29 us -> 0.97 us
where the time goes in v4:
time: 40 us; the launch traced here: 39.9 us
  Pallas kernels  38.9 us (97%)
  local copies, waits for them, and re-layouts  0.97 us (2%)
    pallas_call x1, Pallas kernels, body(): pl.pallas_call(kernel, out_shape=pltpu.VMEM((2 * CL, D), bf16), in_specs=...  38.9 us
    unnamed x1, local copies, waits for them, and re-layouts  0.97 us

profile of v4, /device:TPU:1, one launch (start us, length us, event | category | flops | bytes accessed | tf_op | source)
XLA Modules:
  0.0 39.9 jit_solution(8347252034961771672)
XLA Ops:
  0.0 38.9 %retro.1 = bf16[128,4096]{1,0:T(8,128)(2,1)S(1)} custom-call(bf16[128,4096]{1,0:T(8,128)(2,1)} %queries.1, bf16[16,128,1024]{2,1,0:T(8,128)(2,1)} %encoded.1, bf16[1024,4096]{1,0:T(8,128)(2,1)} %key_weight.1, bf16[1024,4096]{1,0:T(8,128)(2,1)} %value_weight.1, s32[2,2]{1,0:T(2,128)} %shard.1, s32[2,2]{1,0:T(2,128)} %slot.1), custom_call_target="tpu_custom_call" | custom-call | tf_op jit(solution)/shard_map/retro/pallas_call | solution.py:288
  38.9 1.0 %copy.8 = bf16[128,4096]{1,0:T(8,128)(2,1)} copy(bf16[128,4096]{1,0:T(8,128)(2,1)S(1)} %retro.1) | data formatting | bytes 2097152

commit v5 on v4

--- a/solution.py
+++ b/solution.py
@@ -142,50 +142,70 @@
         brings[c].wait()
         return spread(c, 1, [(partner, far[c].at[core, spot]) for partner in along_v])
 
+    def bundle(c, of):
+        return far[c].at[core, pl.ds(of * SIDE, SIDE)]
+
     def bundles(c, moves):
         wait_all(moves)
-        held = far[c].at[core, pl.ds(u * SIDE, SIDE)]
-        return spread(c, 4, [(partner, held) for partner in along_u])
+        held = bundle(c, u)
+        return spread(c, 4, [(partner, held) for partner in [*along_u, other_core]])
 
     def share(c, moves):
-        wait_all(moves)
-        return spread(c, 7, [(other_core, far[c].at[core])])
-
+        shared = [moves[3]]
+        for i, step in enumerate((3, 1, 2)):
+            moves[i].wait()
+            shared += spread(c, 8 + i, [(other_core, bundle(c, (u + step) % SIDE))])
+        return shared
+
+    ones = [None] * DIRECT + [pieces(DIRECT)]
     load_enc.wait()
     load_wk.start()
     load_wv.start()
-    for ask in asks:
-        ask.wait()
+    wait_all(asks[:5])
 
     def place_in(who, g, owner):
         first, second = req[who, g, 0], req[who, g, 1]
         from_second = jnp.where(second // BLK_SH == owner, second % BLK_SH, 0)
         return jnp.where(first // BLK_SH == owner, first % BLK_SH, from_second)
 
-    places = [[place_in((z + step) % N_DB, g, z) for g in range(2)] for step in (0, 1, 3, 2)]
+    def places(step):
+        return [place_in((z + step) % N_DB, g, z) for g in range(2)]
+
     far_places = [place_in(z, g, (z + 2) % N_DB) for g in range(2)]
     owners = [[req[z, g, j] // BLK_SH for j in range(NB)] for g in range(2)]
-    blocks = []
+    blocks = [[] for _ in CHUNKS]
+
+    def direct(c, i, partner, at):
+        row, rows = sum(CHUNKS[:c]), CHUNKS[c]
+        for g in range(2):
+            send[c][i, g] = enc[at[g], row : row + rows, :]
+        move = pltpu.make_async_remote_copy(
+            src_ref=send[c].at[i], dst_ref=recv[c].at[z],
+            send_sem=blk_send.at[c, i], recv_sem=blk_recv.at[c, i],
+            device_id=partner, device_id_type=MESH,
+        )
+        move.start()
+        blocks[c].append(move)
+
+    near_places = [places(1), places(3)]
+    for c in range(DIRECT):
+        for i, partner in enumerate(near):
+            direct(c, i, partner, near_places[i])
+    ones += [pieces(c) for c in range(DIRECT + 1, n)]
+    wait_all(asks[5:])
+    opposite_places = places(2)
+    for c in range(DIRECT):
+        direct(c, 2, opposite, opposite_places)
+    for c in range(DIRECT, n):
+        for i, partner in enumerate(near):
+            direct(c, i, partner, near_places[i])
+    twos = [None] * DIRECT + [bundles(c, ones[c]) for c in range(DIRECT, n)]
+    own_places = places(0)
     row = 0
     for c, rows in enumerate(CHUNKS):
-        moves = []
-        for i, partner in enumerate([*near, opposite] if c < DIRECT else near):
-            for g in range(2):
-                send[c][i, g] = enc[places[i + 1][g], row : row + rows, :]
-            move = pltpu.make_async_remote_copy(
-                src_ref=send[c].at[i], dst_ref=recv[c].at[z],
-                send_sem=blk_send.at[c, i], recv_sem=blk_recv.at[c, i],
-                device_id=partner, device_id_type=MESH,
-            )
-            move.start()
-            moves.append(move)
         for g in range(2):
-            recv[c][z, g] = enc[places[0][g], row : row + rows, :]
-        blocks.append(moves)
+            recv[c][z, g] = enc[own_places[g], row : row + rows, :]
         row += rows
-
-    ones = [None] * DIRECT + [pieces(c) for c in range(DIRECT, n)]
-    twos = [None] * DIRECT + [bundles(c, ones[c]) for c in range(DIRECT, n)]
 
     load_q.wait()
     give_q.wait()
@@ -312,8 +332,8 @@
             pltpu.SemaphoreType.DMA((2, N_DB)),
             pltpu.SemaphoreType.DMA((n, 3)),
             pltpu.SemaphoreType.DMA((n, 3)),
-            pltpu.SemaphoreType.DMA((n, 8)),
-            pltpu.SemaphoreType.DMA((n, 8)),
+            pltpu.SemaphoreType.DMA((n, 11)),
+            pltpu.SemaphoreType.DMA((n, 11)),
             pltpu.SemaphoreType.DMA((2,)),
             pltpu.SemaphoreType.DMA((2,)),
         ],

time: 40 us -> 38.1 us (0.953)
  Pallas kernels: 38.9 us -> 37 us
    pallas_call x1, Pallas kernels: 38.9 us -> 37 us  [body(): pl.pallas_call(kernel, out_shape=pltpu.VMEM((2 * CL, D), bf16), in_specs=...]
where the time goes in v5:
time: 38.1 us; the launch traced here: 37.9 us
  Pallas kernels  37 us (97%)
  local copies, waits for them, and re-layouts  0.97 us (3%)
    pallas_call x1, Pallas kernels, body(): pl.pallas_call(kernel, out_shape=pltpu.VMEM((2 * CL, D), bf16), in_specs=...  37 us
    unnamed x1, local copies, waits for them, and re-layouts  0.97 us

profile of v5, /device:TPU:1, one launch (start us, length us, event | category | flops | bytes accessed | tf_op | source)
XLA Modules:
  0.0 37.9 jit_solution(5374326108175197341)
XLA Ops:
  0.0 37.0 %retro.1 = bf16[128,4096]{1,0:T(8,128)(2,1)S(1)} custom-call(bf16[128,4096]{1,0:T(8,128)(2,1)} %queries.1, bf16[16,128,1024]{2,1,0:T(8,128)(2,1)} %encoded.1, bf16[1024,4096]{1,0:T(8,128)(2,1)} %key_weight.1, bf16[1024,4096]{1,0:T(8,128)(2,1)} %value_weight.1, s32[2,2]{1,0:T(2,128)} %shard.1, s32[2,2]{1,0:T(2,128)} %slot.1), custom_call_target="tpu_custom_call" | custom-call | tf_op jit(solution)/shard_map/retro/pallas_call | solution.py:308
  37.0 1.0 %copy.8 = bf16[128,4096]{1,0:T(8,128)(2,1)} copy(bf16[128,4096]{1,0:T(8,128)(2,1)S(1)} %retro.1) | data formatting | bytes 2097152

commit v6 on v5

--- a/solution.py
+++ b/solution.py
@@ -24,7 +24,7 @@
 DIRECT = 1
 PLAN = {(0, False): (1,), (1, False): (2,), (2, False): (3,)}
 TILE = 4096
-HEADS = 16
+HEADS = 32
 SCALE = math.log2(math.e) / math.sqrt(HD)
 MESH = pl.DeviceIdType.MESH
 

time: 38.1 us -> 37.9 us (level)
  no operation moved by 1% of the time
where the time goes in v6:
time: 37.9 us; the launch traced here: 37.8 us
  Pallas kernels  36.8 us (97%)
  local copies, waits for them, and re-layouts  0.97 us (3%)
    pallas_call x1, Pallas kernels, body(): pl.pallas_call(kernel, out_shape=pltpu.VMEM((2 * CL, D), bf16), in_specs=...  36.8 us
    unnamed x1, local copies, waits for them, and re-layouts  0.97 us

profile of v6, /device:TPU:1, one launch (start us, length us, event | category | flops | bytes accessed | tf_op | source)
XLA Modules:
  0.0 37.8 jit_solution(18317220893257608846)
XLA Ops:
  0.0 36.8 %retro.1 = bf16[128,4096]{1,0:T(8,128)(2,1)S(1)} custom-call(bf16[128,4096]{1,0:T(8,128)(2,1)} %queries.1, bf16[16,128,1024]{2,1,0:T(8,128)(2,1)} %encoded.1, bf16[1024,4096]{1,0:T(8,128)(2,1)} %key_weight.1, bf16[1024,4096]{1,0:T(8,128)(2,1)} %value_weight.1, s32[2,2]{1,0:T(2,128)} %shard.1, s32[2,2]{1,0:T(2,128)} %slot.1), custom_call_target="tpu_custom_call" | custom-call | tf_op jit(solution)/shard_map/retro/pallas_call | solution.py:308
  36.8 1.0 %copy.8 = bf16[128,4096]{1,0:T(8,128)(2,1)} copy(bf16[128,4096]{1,0:T(8,128)(2,1)S(1)} %retro.1) | data formatting | bytes 2097152
